TPU v7x, 32 devices: a whole 2x2x4 slice. The times are simulated.
32 devices in a mesh: group: 2 (over y), inline: 4 (over z), xline: 4 (over x, core).
Axes of the slice: x: 2, y: 2, z: 4, core: 2. Of those that a mesh axis runs over, the one named last changes fastest.
Arguments:
- volume: bfloat16 [32, 64, 64, 128], P(('group', 'inline'), 'xline'), parts along dimension 0, may hold values from -6 to 6
- first_kernel: bfloat16 [27, 128, 128], P(None, 'xline'), may hold values from -0.109375 to 0.109375
- second_kernel: bfloat16 [27, 128, 128], P(None, 'xline'), may hold values from -0.109375 to 0.109375
- cotangent: bfloat16 [16, 32, 32, 128], P(('group', 'inline'), 'xline'), parts along dimension 0, may hold values from -0.15625 to 0.15625
Outputs:
- latent: bfloat16 [16, 32, 32, 128], P(('group', 'inline'), 'xline'), parts along dimension 0
- first_grad: float32 [884736], P(('group', 'inline', 'xline')), parts along dimension 0
- second_grad: float32 [884736], P(('group', 'inline', 'xline')), parts along dimension 0
There are 2 independent parts, one for each index of `group`. A program takes and returns all parts, laid end to end along the dimension named above; an argument that names none is the same for every part. Nothing has to cross between parts.
All inputs are finite; a program needn't handle non-finite values.
Results may differ from a plain program's by a relative error of at most 0.0049.
Values may be sent and summed in bfloat16 or wider, within the bound.
A program may use at most 64 MiB of HBM per device.

v0:
```python
import jax
import jax.numpy as jnp
from jax import lax
from jax.sharding import PartitionSpec as P


def passed_along(block, axis, distance):
    devices = range(lax.axis_size(axis))
    route = [(i - distance, i) for i in devices if i - distance in devices]
    return lax.ppermute(block, axis, route)


def extended(shard, sides, width):
    for axis, dim in sides:
        count, length = (lax.axis_size(axis), shard.shape[dim])
        up = [(i, (i + 1) % count) for i in range(count - 1)]
        down = [(j, i) for i, j in up]
        last = lax.slice_in_dim(shard, length - width, length, axis=dim)
        initial = lax.slice_in_dim(shard, 0, width, axis=dim)
        before = lax.ppermute(last, axis, up)
        after = lax.ppermute(initial, axis, down)
        shard = jnp.concatenate([before, shard, after], axis=dim)
    return shard


def lower_inline(values):
    return passed_along(values[-1:], "inline", 1)


def lower_xline(values):
    return passed_along(values[:, -1:], "xline", 1)


def add_rims(volume):
    widened = jnp.concatenate([lower_xline(volume), volume], axis=1)
    widened = jnp.concatenate([lower_inline(widened), widened], axis=0)
    return jnp.pad(widened, ((0, 0), (0, 0), (1, 0), (0, 0)))


def with_faces(values):
    padded = extended(values, (("inline", 0), ("xline", 1)), 1)
    return jnp.pad(padded, ((0, 0), (0, 0), (1, 1), (0, 0)))


def strided_taps(padded, rows, cols, depth):
    channels = padded.shape[3]
    pieces = []
    for first in range(3):
        for second in range(3):
            for third in range(3):
                pieces.append(
                    lax.slice(
                        padded,
                        (first, second, third, 0),
                        (
                            first + 2 * rows - 1,
                            second + 2 * cols - 1,
                            third + 2 * depth - 1,
                            channels,
                        ),
                        (2, 2, 2, 1),
                    )
                )
    return jnp.stack(pieces)


def unit_taps(padded, rows, cols, depth):
    pieces = []
    for first in range(3):
        for second in range(3):
            for third in range(3):
                pieces.append(
                    padded[first : first + rows, second : second + cols, third : third + depth]
                )
    return jnp.stack(pieces)


def local(volume, first_kernel, second_kernel, cotangent):
    whole_first, whole_second = (
        lax.all_gather(first_kernel, "xline", axis=1, tiled=True),
        lax.all_gather(second_kernel, "xline", axis=1, tiled=True),
    )
    rows = cotangent.shape[0]
    cols = cotangent.shape[1]
    depth = cotangent.shape[2]
    fine_taps = strided_taps(add_rims(volume), rows, cols, depth)
    pre_first = jnp.einsum(
        "txyzc,tcd->xyzd", fine_taps, whole_first, preferred_element_type=jnp.float32
    )
    hidden = jax.nn.silu(pre_first).astype(jnp.bfloat16)
    hidden_taps = unit_taps(with_faces(hidden), rows, cols, depth)
    latent = jnp.einsum(
        "txyzc,tcd->xyzd", hidden_taps, whole_second, preferred_element_type=jnp.float32
    ).astype(jnp.bfloat16)
    grad_second = jnp.einsum(
        "txyzc,xyzd->tcd", hidden_taps, cotangent, preferred_element_type=jnp.float32
    )
    cot_taps = unit_taps(with_faces(cotangent), rows, cols, depth)
    back_hidden = jnp.einsum(
        "txyzd,tcd->xyzc", cot_taps, whole_second[::-1], preferred_element_type=jnp.float32
    )
    sigma = jax.nn.sigmoid(pre_first)
    back_pre = (back_hidden * sigma * (1.0 + pre_first * (1.0 - sigma))).astype(jnp.bfloat16)
    grad_first = jnp.einsum(
        "txyzc,xyzd->tcd", fine_taps, back_pre, preferred_element_type=jnp.float32
    )
    reduced_first, reduced_second = (
        lax.psum_scatter(
            grad_first.reshape(-1), ("inline", "xline"), scatter_dimension=0, tiled=True
        ),
        lax.psum_scatter(
            grad_second.reshape(-1), ("inline", "xline"), scatter_dimension=0, tiled=True
        ),
    )
    return (latent, reduced_first, reduced_second)


def solution(mesh):
    return jax.shard_map(
        local,
        mesh=mesh,
        in_specs=(
            P(("group", "inline"), "xline", None, None),
            P(None, "xline", None),
            P(None, "xline", None),
            P(("group", "inline"), "xline", None, None),
        ),
        out_specs=(
            P(("group", "inline"), "xline", None, None),
            P(("group", "inline", "xline")),
            P(("group", "inline", "xline")),
        ),
        check_vma=False,
    )
```

profile of v0, /device:TPU:0, one launch (start us, length us, event | category | flops | bytes accessed | tf_op | source)
XLA Modules:
  0.0 339.5 jit_solution(13942740601524838486)
XLA Ops:
  8.2 4.9 %collective-permute-start.6 = (bf16[1,8,32,128]{3,2,1,0:T(8,128)(2,1)S(1)}, bf16[1,8,32,128]{3,2,1,0:T(8,128)(2,1)S(1)}, u32[]{:S(2)}, u32[]{:S(2)}) collective-permute-start(bf16[1,8,32,128]{3,2,1,0:T(8,128)(2,1)S(1)} %get-tuple-element.12), channel_id=1, source_target_pairs={{0,4},{4,8},{8,12},{1,5},{5,9},{9,13},{2,6},{6,10},{10,14},{3,7},{... | collective-permute-start | bytes 196616 | tf_op jit(solution)/shard_map/ppermute | solution.py:20
  16.8 9.7 %all_gather.7 = bf16[27,128,128]{2,1,0:T(8,128)(2,1)S(1)} all-gather(bf16[27,32,128]{2,1,0:T(8,128)(2,1)} %param.6), channel_id=1, replica_groups=mesh['group'=2,'inline'=4,'xline'=4] {'xline'}, dimensions={1}, use_global_device_ids=true | all-gather | bytes 1105920 | tf_op jit(solution)/shard_map/all_gather | solution.py:81
  26.5 11.6 %all_gather.6 = bf16[27,128,128]{2,1,0:T(8,128)(2,1)} all-gather(bf16[27,32,128]{2,1,0:T(8,128)(2,1)} %param.5), channel_id=1, replica_groups=mesh['group'=2,'inline'=4,'xline'=4] {'xline'}, dimensions={1}, use_global_device_ids=true | all-gather | bytes 1105920 | tf_op jit(solution)/shard_map/all_gather | solution.py:80
  54.3 4.9 %slice.311 = bf16[2,8,32,128]{3,2,1,0:T(8,128)(2,1)} slice(bf16[5,17,65,128]{3,2,1,0:T(8,128)(2,1)S(1)} %fusion.6), slice={[0:3:2], [0:15:2], [0:63:2], [0:128:1]} | slice | bytes 262144 | tf_op jit(solution)/shard_map/slice | solution.py:52
  59.3 4.9 %slice.312 = bf16[2,8,32,128]{3,2,1,0:T(8,128)(2,1)} slice(bf16[5,17,65,128]{3,2,1,0:T(8,128)(2,1)S(1)} %fusion.6), slice={[0:3:2], [0:15:2], [1:64:2], [0:128:1]} | slice | bytes 262144 | tf_op jit(solution)/shard_map/slice | solution.py:52
  64.1 4.9 %slice.313 = bf16[2,8,32,128]{3,2,1,0:T(8,128)(2,1)} slice(bf16[5,17,65,128]{3,2,1,0:T(8,128)(2,1)S(1)} %fusion.6), slice={[0:3:2], [0:15:2], [2:65:2], [0:128:1]} | slice | bytes 262144 | tf_op jit(solution)/shard_map/slice | solution.py:52
  73.9 4.9 %slice.315 = bf16[2,8,32,128]{3,2,1,0:T(8,128)(2,1)} slice(bf16[5,17,65,128]{3,2,1,0:T(8,128)(2,1)S(1)} %fusion.6), slice={[0:3:2], [1:16:2], [1:64:2], [0:128:1]} | slice | bytes 262144 | tf_op jit(solution)/shard_map/slice | solution.py:52
  78.8 4.9 %slice.316 = bf16[2,8,32,128]{3,2,1,0:T(8,128)(2,1)} slice(bf16[5,17,65,128]{3,2,1,0:T(8,128)(2,1)S(1)} %fusion.6), slice={[0:3:2], [1:16:2], [2:65:2], [0:128:1]} | slice | bytes 262144 | tf_op jit(solution)/shard_map/slice | solution.py:52
  83.7 5.0 %slice.317 = bf16[2,8,32,128]{3,2,1,0:T(8,128)(2,1)} slice(bf16[5,17,65,128]{3,2,1,0:T(8,128)(2,1)S(1)} %fusion.6), slice={[0:3:2], [2:17:2], [0:63:2], [0:128:1]} | slice | bytes 262144 | tf_op jit(solution)/shard_map/slice | solution.py:52
  88.6 4.9 %slice.318 = bf16[2,8,32,128]{3,2,1,0:T(8,128)(2,1)} slice(bf16[5,17,65,128]{3,2,1,0:T(8,128)(2,1)S(1)} %fusion.6), slice={[0:3:2], [2:17:2], [1:64:2], [0:128:1]} | slice | bytes 262144 | tf_op jit(solution)/shard_map/slice | solution.py:52
  93.6 5.0 %slice.319 = bf16[2,8,32,128]{3,2,1,0:T(8,128)(2,1)} slice(bf16[5,17,65,128]{3,2,1,0:T(8,128)(2,1)S(1)} %fusion.6), slice={[0:3:2], [2:17:2], [2:65:2], [0:128:1]} | slice | bytes 262144 | tf_op jit(solution)/shard_map/slice | solution.py:52
  98.6 4.9 %slice.320 = bf16[2,8,32,128]{3,2,1,0:T(8,128)(2,1)} slice(bf16[5,17,65,128]{3,2,1,0:T(8,128)(2,1)S(1)} %fusion.6), slice={[1:4:2], [0:15:2], [0:63:2], [0:128:1]} | slice | bytes 262144 | tf_op jit(solution)/shard_map/slice | solution.py:52
  108.3 4.9 %slice.322 = bf16[2,8,32,128]{3,2,1,0:T(8,128)(2,1)} slice(bf16[5,17,65,128]{3,2,1,0:T(8,128)(2,1)S(1)} %fusion.6), slice={[1:4:2], [0:15:2], [2:65:2], [0:128:1]} | slice | bytes 262144 | tf_op jit(solution)/shard_map/slice | solution.py:52
  118.1 4.9 %slice.324 = bf16[2,8,32,128]{3,2,1,0:T(8,128)(2,1)} slice(bf16[5,17,65,128]{3,2,1,0:T(8,128)(2,1)S(1)} %fusion.6), slice={[1:4:2], [1:16:2], [1:64:2], [0:128:1]} | slice | bytes 262144 | tf_op jit(solution)/shard_map/slice | solution.py:52
  123.0 4.9 %slice.325 = bf16[2,8,32,128]{3,2,1,0:T(8,128)(2,1)} slice(bf16[5,17,65,128]{3,2,1,0:T(8,128)(2,1)S(1)} %fusion.6), slice={[1:4:2], [1:16:2], [2:65:2], [0:128:1]} | slice | bytes 262144 | tf_op jit(solution)/shard_map/slice | solution.py:52
  127.9 5.0 %slice.326 = bf16[2,8,32,128]{3,2,1,0:T(8,128)(2,1)} slice(bf16[5,17,65,128]{3,2,1,0:T(8,128)(2,1)S(1)} %fusion.6), slice={[1:4:2], [2:17:2], [0:63:2], [0:128:1]} | slice | bytes 262144 | tf_op jit(solution)/shard_map/slice | solution.py:52
  132.9 4.9 %slice.327 = bf16[2,8,32,128]{3,2,1,0:T(8,128)(2,1)} slice(bf16[5,17,65,128]{3,2,1,0:T(8,128)(2,1)S(1)} %fusion.6), slice={[1:4:2], [2:17:2], [1:64:2], [0:128:1]} | slice | bytes 262144 | tf_op jit(solution)/shard_map/slice | solution.py:52
  137.8 5.0 %slice.328 = bf16[2,8,32,128]{3,2,1,0:T(8,128)(2,1)} slice(bf16[5,17,65,128]{3,2,1,0:T(8,128)(2,1)S(1)} %fusion.6), slice={[1:4:2], [2:17:2], [2:65:2], [0:128:1]} | slice | bytes 262144 | tf_op jit(solution)/shard_map/slice | solution.py:52
  152.6 4.9 %slice.331 = bf16[2,8,32,128]{3,2,1,0:T(8,128)(2,1)} slice(bf16[5,17,65,128]{3,2,1,0:T(8,128)(2,1)S(1)} %fusion.6), slice={[2:5:2], [0:15:2], [2:65:2], [0:128:1]} | slice | bytes 262144 | tf_op jit(solution)/shard_map/slice | solution.py:52
  167.2 4.9 %slice.334 = bf16[2,8,32,128]{3,2,1,0:T(8,128)(2,1)} slice(bf16[5,17,65,128]{3,2,1,0:T(8,128)(2,1)S(1)} %fusion.6), slice={[2:5:2], [1:16:2], [2:65:2], [0:128:1]} | slice | bytes 262144 | tf_op jit(solution)/shard_map/slice | solution.py:52
  172.1 4.9 %slice.335 = bf16[2,8,32,128]{3,2,1,0:T(8,128)(2,1)} slice(bf16[5,17,65,128]{3,2,1,0:T(8,128)(2,1)S(1)} %fusion.6), slice={[2:5:2], [2:17:2], [0:63:2], [0:128:1]} | slice | bytes 262144 | tf_op jit(solution)/shard_map/slice | solution.py:52
  177.0 5.0 %slice.336 = bf16[2,8,32,128]{3,2,1,0:T(8,128)(2,1)} slice(bf16[5,17,65,128]{3,2,1,0:T(8,128)(2,1)S(1)} %fusion.6), slice={[2:5:2], [2:17:2], [1:64:2], [0:128:1]} | slice | bytes 262144 | tf_op jit(solution)/shard_map/slice | solution.py:52
  182.0 5.0 %slice.337 = bf16[2,8,32,128]{3,2,1,0:T(8,128)(2,1)} slice(bf16[5,17,65,128]{3,2,1,0:T(8,128)(2,1)S(1)} %fusion.6), slice={[2:5:2], [2:17:2], [2:65:2], [0:128:1]} | slice | bytes 262144 | tf_op jit(solution)/shard_map/slice | solution.py:52
  226.7 102.9 %all-reduce.8.cloned.1.call-done = (f32[442368]{0:T(1024)}, f32[442368]{0:T(1024)}) async-done(((f32[442368]{0:T(1024)}, f32[442368]{0:T(1024)}), (f32[442368]{0:T(1024)}, f32[442368]{0:T(1024)})) %all-reduce.8.cloned.1.call-update) | async-done | bytes 3538960
  (174 shorter events, 96.2 us)
Async XLA Ops:
  7.2 31.0 %copy-start = (bf16[2,8,32,128]{3,2,1,0:T(8,128)(2,1)S(1)}, bf16[2,8,32,128]{3,2,1,0:T(8,128)(2,1)}, u32[]{:S(2)}) copy-start(bf16[2,8,32,128]{3,2,1,0:T(8,128)(2,1)} %param.7) | copy-start | bytes 393220
  7.2 34.7 %copy-start.1 = (bf16[4,16,64,128]{3,2,1,0:T(8,128)(2,1)S(1)}, bf16[4,16,64,128]{3,2,1,0:T(8,128)(2,1)}, u32[]{:S(2)}) copy-start(bf16[4,16,64,128]{3,2,1,0:T(8,128)(2,1)} %param.4) | copy-start | bytes 3145732
  7.2 322.4 %all-reduce.8.cloned.1.call-start = ((), (), s32[]{:S(2)}) async-start(), calls=%async_computation | async-start | bytes 7077888
  8.2 30.0 %collective-permute-start.6 = (bf16[1,8,32,128]{3,2,1,0:T(8,128)(2,1)S(1)}, bf16[1,8,32,128]{3,2,1,0:T(8,128)(2,1)S(1)}, u32[]{:S(2)}, u32[]{:S(2)}) collective-permute-start(bf16[1,8,32,128]{3,2,1,0:T(8,128)(2,1)S(1)} %get-tuple-element.12), channel_id=1, source_target_pairs={{0,4},{4,8},{8,12},{1,5},{5,9},{9,13},{2,6},{6,10},{10,14},{3,7},{... | collective-permute-start | bytes 196616 | tf_op jit(solution)/shard_map/ppermute | solution.py:20
  13.1 25.1 %collective-permute-start.7 = (bf16[1,8,32,128]{3,2,1,0:T(8,128)(2,1)S(1)}, bf16[1,8,32,128]{3,2,1,0:T(8,128)(2,1)S(1)}, u32[]{:S(2)}, u32[]{:S(2)}) collective-permute-start(bf16[1,8,32,128]{3,2,1,0:T(8,128)(2,1)S(1)} %get-tuple-element.11), channel_id=1, source_target_pairs={{4,0},{8,4},{12,8},{5,1},{9,5},{13,9},{6,2},{10,6},{14,10},{7,3},{... | collective-permute-start | bytes 196616 | tf_op jit(solution)/shard_map/ppermute | solution.py:21
  15.3 26.5 %collective-permute-start = (bf16[4,1,64,128]{3,2,1,0:T(8,128)(2,1)S(1)}, bf16[4,1,64,128]{3,2,1,0:T(8,128)(2,1)S(1)}, u32[]{:S(2)}, u32[]{:S(2)}) collective-permute-start(bf16[4,1,64,128]{3,2,1,0:T(8,128)(2,1)S(1)} %slice.309), channel_id=1, source_target_pairs={{0,1},{1,2},{2,3},{4,5},{5,6},{6,7},{8,9},{9,10},{10,11},{12,13},{... | collective-permute-start | bytes 196616 | tf_op jit(solution)/shard_map/ppermute | solution.py:10
  38.3 8.3 %collective-permute-start.8 = (bf16[4,1,32,128]{3,2,1,0:T(8,128)(2,1)S(1)}, bf16[4,1,32,128]{3,2,1,0:T(8,128)(2,1)S(1)}, u32[]{:S(2)}, u32[]{:S(2)}) collective-permute-start(bf16[4,1,32,128]{3,2,1,0:T(8,128)(2,1)S(1)} %get-tuple-element.5), channel_id=1, source_target_pairs={{0,1},{1,2},{2,3},{4,5},{5,6},{6,7},{8,9},{9,10},{10,11},{12,13},{... | collective-permute-start | bytes 98312 | tf_op jit(solution)/shard_map/ppermute | solution.py:20
  40.5 6.1 %collective-permute-start.9 = (bf16[4,1,32,128]{3,2,1,0:T(8,128)(2,1)S(1)}, bf16[4,1,32,128]{3,2,1,0:T(8,128)(2,1)S(1)}, u32[]{:S(2)}, u32[]{:S(2)}) collective-permute-start(bf16[4,1,32,128]{3,2,1,0:T(8,128)(2,1)S(1)} %get-tuple-element.6), channel_id=1, source_target_pairs={{1,0},{2,1},{3,2},{5,4},{6,5},{7,6},{9,8},{10,9},{11,10},{13,12},{... | collective-permute-start | bytes 98312 | tf_op jit(solution)/shard_map/ppermute | solution.py:21
  42.0 11.4 %collective-permute-start.1 = (bf16[1,17,64,128]{3,2,1,0:T(8,128)(2,1)S(1)}, bf16[1,17,64,128]{3,2,1,0:T(8,128)(2,1)S(1)}, u32[]{:S(2)}, u32[]{:S(2)}) collective-permute-start(bf16[1,17,64,128]{3,2,1,0:T(8,128)(2,1)S(1)} %slice.398), channel_id=1, source_target_pairs={{0,4},{4,8},{8,12},{1,5},{5,9},{9,13},{2,6},{6,10},{10,14},{3,7},{... | collective-permute-start | bytes 835592 | tf_op jit(solution)/shard_map/ppermute | solution.py:10
  187.0 13.3 %copy-start.12 = (bf16[2,8,32,128]{3,2,1,0:T(8,128)(2,1)S(1)}, bf16[2,8,32,128]{3,2,1,0:T(8,128)(2,1)}, u32[]{:S(2)}) copy-start(bf16[2,8,32,128]{3,2,1,0:T(8,128)(2,1)} %slice.328) | copy-start | bytes 393220
  187.0 13.4 %copy-start.11 = (bf16[2,8,32,128]{3,2,1,0:T(8,128)(2,1)S(1)}, bf16[2,8,32,128]{3,2,1,0:T(8,128)(2,1)}, u32[]{:S(2)}) copy-start(bf16[2,8,32,128]{3,2,1,0:T(8,128)(2,1)} %slice.329) | copy-start | bytes 393220
  187.0 13.4 %copy-start.10 = (bf16[2,8,32,128]{3,2,1,0:T(8,128)(2,1)S(1)}, bf16[2,8,32,128]{3,2,1,0:T(8,128)(2,1)}, u32[]{:S(2)}) copy-start(bf16[2,8,32,128]{3,2,1,0:T(8,128)(2,1)} %slice.330) | copy-start | bytes 393220
  187.0 13.4 %copy-start.9 = (bf16[2,8,32,128]{3,2,1,0:T(8,128)(2,1)S(1)}, bf16[2,8,32,128]{3,2,1,0:T(8,128)(2,1)}, u32[]{:S(2)}) copy-start(bf16[2,8,32,128]{3,2,1,0:T(8,128)(2,1)} %slice.331) | copy-start | bytes 393220
  187.1 13.5 %copy-start.8 = (bf16[2,8,32,128]{3,2,1,0:T(8,128)(2,1)S(1)}, bf16[2,8,32,128]{3,2,1,0:T(8,128)(2,1)}, u32[]{:S(2)}) copy-start(bf16[2,8,32,128]{3,2,1,0:T(8,128)(2,1)} %slice.332) | copy-start | bytes 393220
  187.1 13.5 %copy-start.7 = (bf16[2,8,32,128]{3,2,1,0:T(8,128)(2,1)S(1)}, bf16[2,8,32,128]{3,2,1,0:T(8,128)(2,1)}, u32[]{:S(2)}) copy-start(bf16[2,8,32,128]{3,2,1,0:T(8,128)(2,1)} %slice.333) | copy-start | bytes 393220
  187.1 13.5 %copy-start.6 = (bf16[2,8,32,128]{3,2,1,0:T(8,128)(2,1)S(1)}, bf16[2,8,32,128]{3,2,1,0:T(8,128)(2,1)}, u32[]{:S(2)}) copy-start(bf16[2,8,32,128]{3,2,1,0:T(8,128)(2,1)} %slice.334) | copy-start | bytes 393220
  187.1 13.5 %copy-start.5 = (bf16[2,8,32,128]{3,2,1,0:T(8,128)(2,1)S(1)}, bf16[2,8,32,128]{3,2,1,0:T(8,128)(2,1)}, u32[]{:S(2)}) copy-start(bf16[2,8,32,128]{3,2,1,0:T(8,128)(2,1)} %slice.335) | copy-start | bytes 393220
  187.1 13.6 %copy-start.4 = (bf16[2,8,32,128]{3,2,1,0:T(8,128)(2,1)S(1)}, bf16[2,8,32,128]{3,2,1,0:T(8,128)(2,1)}, u32[]{:S(2)}) copy-start(bf16[2,8,32,128]{3,2,1,0:T(8,128)(2,1)} %slice.336) | copy-start | bytes 393220
  187.1 13.6 %copy-start.3 = (bf16[2,8,32,128]{3,2,1,0:T(8,128)(2,1)S(1)}, bf16[2,8,32,128]{3,2,1,0:T(8,128)(2,1)}, u32[]{:S(2)}) copy-start(bf16[2,8,32,128]{3,2,1,0:T(8,128)(2,1)} %slice.337) | copy-start | bytes 393220
  187.1 13.6 %copy-start.2 = (bf16[27,128,128]{2,1,0:T(8,128)(2,1)S(1)}, bf16[27,128,128]{2,1,0:T(8,128)(2,1)}, u32[]{:S(2)}) copy-start(bf16[27,128,128]{2,1,0:T(8,128)(2,1)} %all_gather.6) | copy-start | bytes 2654212
  201.9 6.8 %collective-permute-start.2 = (bf16[1,8,32,128]{3,2,1,0:T(8,128)(2,1)S(1)}, bf16[1,8,32,128]{3,2,1,0:T(8,128)(2,1)S(1)}, u32[]{:S(2)}, u32[]{:S(2)}) collective-permute-start(bf16[1,8,32,128]{3,2,1,0:T(8,128)(2,1)S(1)} %get-tuple-element.13), channel_id=1, source_target_pairs={{0,4},{4,8},{8,12},{1,5},{5,9},{9,13},{2,6},{6,10},{10,14},{3,7},{... | collective-permute-start | bytes 196616 | tf_op jit(solution)/shard_map/ppermute | solution.py:20
  206.3 6.2 %collective-permute-start.3 = (bf16[1,8,32,128]{3,2,1,0:T(8,128)(2,1)S(1)}, bf16[1,8,32,128]{3,2,1,0:T(8,128)(2,1)S(1)}, u32[]{:S(2)}, u32[]{:S(2)}) collective-permute-start(bf16[1,8,32,128]{3,2,1,0:T(8,128)(2,1)S(1)} %get-tuple-element.14), channel_id=1, source_target_pairs={{4,0},{8,4},{12,8},{5,1},{9,5},{13,9},{6,2},{10,6},{14,10},{7,3},{... | collective-permute-start | bytes 196616 | tf_op jit(solution)/shard_map/ppermute | solution.py:21
  212.4 5.0 %collective-permute-start.4 = (bf16[4,1,32,128]{3,2,1,0:T(8,128)(2,1)S(1)}, bf16[4,1,32,128]{3,2,1,0:T(8,128)(2,1)S(1)}, u32[]{:S(2)}, u32[]{:S(2)}) collective-permute-start(bf16[4,1,32,128]{3,2,1,0:T(8,128)(2,1)S(1)} %get-tuple-element.9), channel_id=1, source_target_pairs={{0,1},{1,2},{2,3},{4,5},{5,6},{6,7},{8,9},{9,10},{10,11},{12,13},{... | collective-permute-start | bytes 98312 | tf_op jit(solution)/shard_map/ppermute | solution.py:20
  213.7 3.7 %collective-permute-start.5 = (bf16[4,1,32,128]{3,2,1,0:T(8,128)(2,1)S(1)}, bf16[4,1,32,128]{3,2,1,0:T(8,128)(2,1)S(1)}, u32[]{:S(2)}, u32[]{:S(2)}) collective-permute-start(bf16[4,1,32,128]{3,2,1,0:T(8,128)(2,1)S(1)} %get-tuple-element.10), channel_id=1, source_target_pairs={{1,0},{2,1},{3,2},{5,4},{6,5},{7,6},{9,8},{10,9},{11,10},{13,12},{... | collective-permute-start | bytes 98312 | tf_op jit(solution)/shard_map/ppermute | solution.py:21
  (7 other events, 51.5 us)
Sparse Core Ops, SparseCore 0:
  221.2 108.3 all-reduce.7
where the time goes:
time: 340 us
  local copies, waits for them, and re-layouts  156 us (46%)
  waiting for transfers between devices  111 us (33%)
  starting transfers between devices  24.1 us (7%)
  blocking collectives  21.3 us (6%)
  between operations  15.6 us (5%)
  matrix products  10 us (3%)
    slice x27, local copies, waits for them, and re-layouts, strided_taps(): lax.slice(padded, (first, second, third, 0), (first + 2 * rows - 1, secon...  133 us
    unnamed x2, waiting for transfers between devices  103 us
    unnamed x114, local copies, waits for them, and re-layouts  20.8 us
    ppermute x4, starting transfers between devices, extended(): before = lax.ppermute(last, axis, up)  12.9 us
    all_gather x1, blocking collectives, local(): lax.all_gather(first_kernel, 'xline', axis=1, tiled=True)  11.6 us
    all_gather x1, blocking collectives, local(): lax.all_gather(second_kernel, 'xline', axis=1, tiled=True)  9.75 us
  transfers between devices with their start and end apart: 11, of which 3 were waited for; matrix products, arithmetic and copies ran while one was open for 3% of the time, Pallas kernels for 0%

commit v1 on v0

v1 whole, which is shorter than its diff:
```python
import functools
import itertools

import jax
import jax.numpy as jnp
from jax import lax
from jax.experimental import pallas as pl
from jax.experimental.pallas import tpu as pltpu
from jax.sharding import PartitionSpec as P

F32 = jnp.float32
BF16 = jnp.bfloat16
MESH = pl.DeviceIdType.MESH
TAPS = 27
LANES = 128
ALL_WAYS = [d for d in itertools.product((-1, 0, 1), repeat=2) if d != (0, 0)]
UP_WAYS = [(1, 0), (0, 1), (1, 1)]


def dot(left, right, dims=((1,), (0,))):
    return lax.dot_general(left, right, (dims, ((), ())), preferred_element_type=F32)


def remote(src, dst, send, recv, device):
    return pltpu.make_async_remote_copy(
        src_ref=src, dst_ref=dst, send_sem=send, recv_sem=recv,
        device_id=device, device_id_type=MESH,
    )


class Rim:
    def __init__(self, own, padded, low, send, recv, ways, place):
        inline, xline, inlines, xlines = place
        rows, cols = own.shape[0], own.shape[1]
        self.padded = padded
        self.items = []
        for n, (di, dx) in enumerate(ways):
            def there(si, sx, place=place):
                ok = None
                for step, at, count in ((si, inline, inlines), (sx, xline, xlines)):
                    if step == 1:
                        one = at < count - 1
                    elif step == -1:
                        one = at > 0
                    else:
                        continue
                    ok = one if ok is None else jnp.logical_and(ok, one)
                return ok

            def source(step, count):
                return {1: pl.ds(count - 1, 1), -1: pl.ds(0, 1), 0: pl.ds(0, count)}[step]

            def target(step, count):
                return {1: pl.ds(0, 1), -1: pl.ds(low + count, 1), 0: pl.ds(low, count)}[step]

            spot = (target(di, rows), target(dx, cols))
            copy = remote(
                own.at[source(di, rows), source(dx, cols)],
                padded.at[spot[0], spot[1]],
                send.at[n],
                recv.at[n],
                {
                    "inline": lax.rem(inline + di + inlines, inlines),
                    "xline": lax.rem(xline + dx + xlines, xlines),
                },
            )
            self.items.append((copy, spot, there(di, dx), there(-di, -dx)))

    def start(self):
        for copy, _, sends, _ in self.items:
            pl.when(sends)(copy.start)

    def clear(self):
        for _, spot, _, gets in self.items:
            @pl.when(jnp.logical_not(gets))
            def _():
                shape = (spot[0].size, spot[1].size) + tuple(self.padded.shape[2:])
                self.padded[spot[0], spot[1]] = jnp.zeros(shape, self.padded.dtype)

    def arrive(self):
        for copy, _, _, gets in self.items:
            pl.when(gets)(copy.wait_recv)

    def sent(self):
        for copy, _, sends, _ in self.items:
            pl.when(sends)(copy.wait_send)


class Spread:
    def __init__(self, shard, whole, sems, place):
        _, xline, _, _ = place
        send, recv, local = sems
        width = shard.shape[1]
        near = xline + 1 - 2 * lax.rem(xline, 2)
        far = lax.rem(xline + 2, 4)

        def part(index):
            return whole.at[:, pl.ds(pl.multiple_of(index * width, width), width), :]

        self.own = pltpu.make_async_copy(shard, part(xline), local)
        self.far = remote(shard, part(xline), send.at[0], recv.at[0], {"xline": far})
        self.near = remote(shard, part(xline), send.at[1], recv.at[1], {"xline": near})
        self.pass_on = remote(part(far), part(far), send.at[2], recv.at[2], {"xline": near})

    def start(self):
        self.far.start()
        self.near.start()
        self.own.start()

    def forward(self):
        self.far.wait_recv()
        self.pass_on.start()

    def arrive(self):
        self.own.wait()
        self.near.wait_recv()
        self.pass_on.wait_recv()

    def sent(self):
        self.far.wait_send()
        self.near.wait_send()
        self.pass_on.wait_send()


class Scatter:
    def __init__(self, total, bufs, sems, place):
        inline, xline, inlines, _ = place
        self.total, self.place = total, place
        self.p, self.r1, self.q, self.r2, self.s, self.r3 = bufs
        send, recv = sems
        self.core, self.x = lax.rem(xline, 2), xline // 2
        near = xline + 1 - 2 * self.core
        far = lax.rem(xline + 2, 4)
        self.rows = TAPS * LANES // (4 * inlines)
        self.one = remote(self.p.at[1 - self.core], self.r1, send.at[0], recv.at[0], {"xline": near})
        self.two = remote(self.q.at[1 - self.x], self.r2, send.at[1], recv.at[1], {"xline": far})
        self.three = []
        for d in range(1, inlines):
            to = lax.rem(inline + d, inlines)
            self.three.append(
                remote(self.s.at[to], self.r3.at[d - 1], send.at[1 + d], recv.at[1 + d], {"inline": to})
            )

    def first(self):
        slot_rows = self.p.shape[3]
        for slot in range(4 * self.place[2]):
            self.p[slot % 2, slot // 2 % 2, slot // 4] = self.total[
                pl.ds(slot * self.rows, slot_rows), :
            ].astype(BF16)
        self.one.start()

    def second(self):
        self.one.wait_recv()
        for x in range(2):
            self.q[x] = (self.p[self.core, x].astype(F32) + self.r1[x].astype(F32)).astype(BF16)
        self.two.start()

    def third(self):
        self.two.wait_recv()
        self.s[...] = (self.q[self.x].astype(F32) + self.r2[...].astype(F32)).astype(BF16)
        for copy in self.three:
            copy.start()

    def last(self, out):
        inline = self.place[0]
        total = self.q[self.x, inline].astype(F32) + self.r2[inline].astype(F32)
        for n, copy in enumerate(self.three):
            copy.wait_recv()
            total = total + self.r3[n].astype(F32)
        out[...] = total[: self.rows]

    def sent(self):
        self.one.wait_send()
        self.two.wait_send()
        for copy in self.three:
            copy.wait_send()


def spread_depth(padded, wide, turned, shape):
    rows, cols, depth = shape
    for pi in range(rows + 2):
        cells = padded[pi].astype(F32)
        edge = jnp.zeros((cols + 2, 1, LANES), F32)
        before = jnp.concatenate([edge, cells[:, : depth - 1]], axis=1)
        after = jnp.concatenate([cells[:, 1:], edge], axis=1)
        order = (after, cells, before) if turned else (before, cells, after)
        for c in range(3):
            wide[pi, :, :, c * LANES : (c + 1) * LANES] = order[c].astype(BF16)


def kernel(
    sizes, fused,
    vol, k1, k2, cot, latent, out1, out2,
    vpad, vwide, fine, cpad, cwide, hpad, hwide, w1, w2, pre, bpre, g1, g2,
    vs, vr, cs, cr, hs, hr, w1s, w1r, w1l, w2s, w2r, w2l, *rest,
):
    inlines, xlines = sizes
    inline, xline = lax.axis_index("inline"), lax.axis_index("xline")
    place = (inline, xline, inlines, xlines)
    rows, cols, depth = cot.shape[0], cot.shape[1], cot.shape[2]
    count = cols * depth

    barrier = pltpu.get_barrier_semaphore()
    if fused:
        for di in range(inlines):
            for dx in range(xlines):
                if di or dx:
                    pl.semaphore_signal(
                        barrier, inc=1, device_id_type=MESH,
                        device_id={
                            "inline": lax.rem(inline + di, inlines),
                            "xline": lax.rem(xline + dx, xlines),
                        },
                    )
        pl.semaphore_wait(barrier, inlines * xlines - 1)
    else:
        def greet(di, first):
            for dx in range(first, xlines):
                pl.semaphore_signal(
                    barrier, inc=1, device_id_type=MESH,
                    device_id={
                        "inline": lax.rem(inline + di + inlines, inlines),
                        "xline": lax.rem(xline + dx, xlines),
                    },
                )

        greet(0, 1)
        pl.semaphore_wait(barrier, xlines - 1)
        for di, has in ((1, inline < inlines - 1), (-1, inline > 0)):
            pl.when(has)(functools.partial(greet, di, 0))
        for has in (inline < inlines - 1, inline > 0):
            @pl.when(has)
            def _():
                pl.semaphore_wait(barrier, xlines)

    volume_rim = Rim(vol, vpad, 1, vs, vr, UP_WAYS, place)
    cot_rim = Rim(cot, cpad, 1, cs, cr, ALL_WAYS, place)
    first = Spread(k1, w1, (w1s, w1r, w1l), place)
    second = Spread(k2, w2, (w2s, w2r, w2l), place)
    volume_rim.start()
    first.start()
    cot_rim.start()
    second.start()

    volume_rim.clear()
    cot_rim.clear()
    cpad[1 : rows + 1, 1 : cols + 1] = cot[...]
    fine[:, 0:8, :] = jnp.zeros((fine.shape[0], 8, LANES), F32)

    def split(plane, index, py):
        for c in range(3):
            vwide[index, py % 2, py // 2, :, c * LANES : (c + 1) * LANES] = plane[
                py, pl.ds(7 + c, depth, stride=2), :
            ].astype(BF16)

    def own_plane(index, carry):
        fine[1 : 2 * cols + 1, 8:, :] = vol[index].astype(F32)
        for py in range(1, 2 * cols + 1):
            split(fine, index + 1, py)
        return carry

    lax.fori_loop(0, 2 * rows, own_plane, 0)
    volume_rim.arrive()
    fine[0 : 2 * cols + 1, 8:, :] = vpad[0].astype(F32)
    for py in range(2 * cols + 1):
        split(fine, 0, py)
    for px in range(1, 2 * rows + 1):
        fine[px, 8:, :] = vpad[px, 0].astype(F32)
        for c in range(3):
            vwide[px, 0, 0, :, c * LANES : (c + 1) * LANES] = fine[
                px, pl.ds(7 + c, depth, stride=2), :
            ].astype(BF16)

    cot_rim.arrive()
    spread_depth(cpad, cwide, True, (rows, cols, depth))

    def fine_taps(i, a, b):
        return vwide[2 * i + a, b % 2, pl.ds(b // 2, cols)].reshape(count, 3 * LANES)

    def unit_taps(wide, i, a, b):
        return wide[i + a, pl.ds(b, cols)].reshape(count, 3 * LANES)

    steps = list(itertools.product(range(3), repeat=2))

    first.forward()
    first.arrive()
    for i in range(rows):
        total = jnp.zeros((count, LANES), F32)
        for a, b in steps:
            taps = w1[pl.ds(9 * a + 3 * b, 3)].reshape(3 * LANES, LANES)
            total = total + dot(fine_taps(i, a, b), taps)
        pre[i] = total
        hidden = (total / (1.0 + jnp.exp(-total))).astype(BF16)
        hpad[i + 1, 1 : cols + 1] = hidden.reshape(cols, depth, LANES)
    hidden_own = hpad.at[pl.ds(1, rows), pl.ds(1, cols)]
    hidden_rim = Rim(hidden_own, hpad, 1, hs, hr, ALL_WAYS, place)
    hidden_rim.start()
    hidden_rim.clear()
    second.forward()

    if fused:
        bufs, sems = rest[:12], rest[12:]
        sum2 = Scatter(g2, bufs[:6], sems[:2], place)
        sum1 = Scatter(g1, bufs[6:], sems[2:], place)
        pad = g1.shape[0] - TAPS * LANES
        for g in (g1, g2):
            g[TAPS * LANES :, :] = jnp.zeros((pad, LANES), F32)

    turned = [
        hpad[i + 1, 1 : cols + 1].reshape(count, LANES).astype(F32).T.astype(BF16)
        for i in range(rows)
    ]
    for a, b in steps:
        total = jnp.zeros((LANES, 3 * LANES), F32)
        for i in range(rows):
            total = total + dot(turned[i], unit_taps(cwide, i, 2 - a, 2 - b))
        for c in range(3):
            g2[pl.ds((9 * a + 3 * b + c) * LANES, LANES), :] = total[:, c * LANES : (c + 1) * LANES]
    if fused:
        sum2.first()

    second.arrive()
    for i in range(rows):
        total = jnp.zeros((count, LANES), F32)
        for a, b in steps:
            for c in range(3):
                cells = cwide[
                    i + 2 - a, pl.ds(2 - b, cols), :, c * LANES : (c + 1) * LANES
                ].reshape(count, LANES)
                total = total + dot(cells, w2[9 * a + 3 * b + c], ((1,), (1,)))
        value = pre[i]
        sigma = 1.0 / (1.0 + jnp.exp(-value))
        bpre[i] = (total * sigma * (1.0 + value * (1.0 - sigma))).astype(BF16)
    if fused:
        sum2.second()

    for a, b in steps:
        total = jnp.zeros((3 * LANES, LANES), F32)
        for i in range(rows):
            total = total + dot(fine_taps(i, a, b), bpre[i], ((0,), (0,)))
        g1[pl.ds((9 * a + 3 * b) * LANES, 3 * LANES), :] = total
    if fused:
        sum1.first()
        sum2.third()

    hidden_rim.arrive()
    spread_depth(hpad, hwide, False, (rows, cols, depth))
    if fused:
        sum1.second()
    for i in range(rows):
        total = jnp.zeros((count, LANES), F32)
        for a, b in steps:
            taps = w2[pl.ds(9 * a + 3 * b, 3)].reshape(3 * LANES, LANES)
            total = total + dot(unit_taps(hwide, i, a, b), taps)
        latent[i] = total.astype(BF16).reshape(cols, depth, LANES)

    if fused:
        sum1.third()
        sum2.last(out2)
        sum1.last(out1)
        sum1.sent()
        sum2.sent()
    else:
        out1[...] = g1[: TAPS * LANES]
        out2[...] = g2[: TAPS * LANES]
    for group in (volume_rim, cot_rim, hidden_rim, first, second):
        group.sent()


def local(volume, first_kernel, second_kernel, cotangent):
    inlines, xlines = lax.axis_size("inline"), lax.axis_size("xline")
    rows, cols, depth, channels = cotangent.shape
    shards = inlines * xlines
    fused = inlines <= 4 and (TAPS * LANES) % (8 * shards) == 0
    out_rows = TAPS * LANES // shards if fused else TAPS * LANES
    slot = -(-out_rows // 16) * 16
    dma = pltpu.SemaphoreType.DMA
    pad_cells = (rows + 2, cols + 2, depth)
    scratch = [
        pltpu.VMEM((2 * rows + 1, 2 * cols + 1, 2 * depth, channels), BF16),
        pltpu.VMEM((2 * rows + 1, 2, cols + 1, depth, 3 * channels), BF16),
        pltpu.VMEM((2 * cols + 1, 2 * depth + 8, channels), F32),
        pltpu.VMEM(pad_cells + (channels,), BF16),
        pltpu.VMEM(pad_cells + (3 * channels,), BF16),
        pltpu.VMEM(pad_cells + (channels,), BF16),
        pltpu.VMEM(pad_cells + (3 * channels,), BF16),
        pltpu.VMEM((TAPS, channels, channels), BF16),
        pltpu.VMEM((TAPS, channels, channels), BF16),
        pltpu.VMEM((rows, cols * depth, channels), F32),
        pltpu.VMEM((rows, cols * depth, channels), BF16),
        pltpu.VMEM((TAPS * channels + 8, channels), F32),
        pltpu.VMEM((TAPS * channels + 8, channels), F32),
        dma((3,)), dma((3,)), dma((8,)), dma((8,)), dma((8,)), dma((8,)),
        dma((3,)), dma((3,)), dma, dma((3,)), dma((3,)), dma,
    ]
    if fused:
        for _ in range(2):
            scratch += [
                pltpu.VMEM((2, 2, inlines, slot, channels), BF16),
                pltpu.VMEM((2, inlines, slot, channels), BF16),
                pltpu.VMEM((2, inlines, slot, channels), BF16),
                pltpu.VMEM((inlines, slot, channels), BF16),
                pltpu.VMEM((inlines, slot, channels), BF16),
                pltpu.VMEM((max(inlines - 1, 1), slot, channels), BF16),
            ]
        scratch += [dma((inlines + 1,))] * 4
    flops = 10 * TAPS * channels * channels * rows * cols * depth
    latent, grad1, grad2 = pl.pallas_call(
        functools.partial(kernel, (inlines, xlines), fused),
        out_shape=[
            jax.ShapeDtypeStruct(cotangent.shape, BF16),
            jax.ShapeDtypeStruct((out_rows, channels), F32),
            jax.ShapeDtypeStruct((out_rows, channels), F32),
        ],
        in_specs=[pl.BlockSpec(memory_space=pltpu.VMEM)] * 4,
        out_specs=[pl.BlockSpec(memory_space=pltpu.VMEM)] * 3,
        scratch_shapes=scratch,
        cost_estimate=pl.CostEstimate(flops=flops, bytes_accessed=4 << 20, transcendentals=0),
        compiler_params=pltpu.CompilerParams(
            collective_id=0, has_side_effects=True, vmem_limit_bytes=48 << 20
        ),
    )(volume, first_kernel, second_kernel, cotangent)
    grads = [grad1.reshape(-1), grad2.reshape(-1)]
    if not fused:
        grads = [
            lax.psum_scatter(g, ("inline", "xline"), scatter_dimension=0, tiled=True) for g in grads
        ]
    return latent, grads[0], grads[1]


def solution(mesh):
    return jax.shard_map(
        local,
        mesh=mesh,
        in_specs=(
            P(("group", "inline"), "xline", None, None),
            P(None, "xline", None),
            P(None, "xline", None),
            P(("group", "inline"), "xline", None, None),
        ),
        out_specs=(
            P(("group", "inline"), "xline", None, None),
            P(("group", "inline", "xline")),
            P(("group", "inline", "xline")),
        ),
        check_vma=False,
    )
```

time: 340 us -> 47.3 us (0.14)
  local copies, waits for them, and re-layouts: 156 us -> 5.95 us
  waiting for transfers between devices: 111 us -> 0 us
  Pallas kernels: 0 us -> 40.5 us
  starting transfers between devices: 24.1 us -> 0 us
  blocking collectives: 21.3 us -> 0 us
  between operations: 15.6 us -> 0.65 us
  matrix products: 10 us -> 0 us
    slice x32 -> x0, local copies, waits for them, and re-layouts: 135 us -> none  [the longest x27 133 us: strided_taps(): lax.slice(padded, (first, second, third, 0), (first + 2 * rows - 1, secon...]
    unnamed x2 -> x0, waiting for transfers between devices: 103 us -> none
    pallas_call x0 -> x1, Pallas kernels: none -> 40.5 us  [local(): pl.pallas_call(functools.partial(kernel, (inlines, xlines), fused), out_s...]
    ppermute x10 -> x0, starting transfers between devices: 24 us -> none  [the longest x4 12.9 us: extended(): before = lax.ppermute(last, axis, up)]
    all_gather x2 -> x0, blocking collectives: 21.3 us -> none  [the longest x1 11.6 us: local(): lax.all_gather(first_kernel, 'xline', axis=1, tiled=True)]
    unnamed x114 -> x11, local copies, waits for them, and re-layouts: 20.8 us -> 5.95 us
    dot_general x5 -> x0, matrix products: 10 us -> none  [the longest x1 3.08 us: local(): jnp.einsum('txyzc,tcd->xyzd', hidden_taps, whole_second, preferred_elemen...]
    ppermute x10 -> x0, waiting for transfers between devices: 7.74 us -> none  [the longest x2 3.94 us: passed_along(): return lax.ppermute(block, axis, route)]
  transfers between devices with their start and end apart: 11 -> 0, of which waited for: 3 -> 0; matrix products, arithmetic and copies ran while one was open for 3% -> 0% of each run, Pallas kernels for 0% -> 0%
where the time goes in v1:
time: 47.3 us; the launch traced here: 47.1 us
  Pallas kernels  40.5 us (86%)
  local copies, waits for them, and re-layouts  5.95 us (13%)
  between operations  0.65 us (1%)
    pallas_call x1, Pallas kernels, local(): pl.pallas_call(functools.partial(kernel, (inlines, xlines), fused), out_s...  40.5 us
    unnamed x11, local copies, waits for them, and re-layouts  5.95 us

profile of v1, /device:TPU:0, one launch (start us, length us, event | category | flops | bytes accessed | tf_op | source)
XLA Modules:
  0.0 47.1 jit_solution(7170101961936889273)
XLA Ops:
  0.6 0.0 copy-start
  0.6 1.2 %copy-done = bf16[4,16,64,128]{3,2,1,0:T(8,128)(2,1)S(1)} copy-done((bf16[4,16,64,128]{3,2,1,0:T(8,128)(2,1)S(1)}, bf16[4,16,64,128]{3,2,1,0:T(8,128)(2,1)}, u32[]{:S(2)}) %copy-start) | copy-done | bytes 1048600
  1.9 0.0 copy-start.1
  1.9 0.9 %copy-done.1 = bf16[27,32,128]{2,1,0:T(8,128)(2,1)S(1)} copy-done((bf16[27,32,128]{2,1,0:T(8,128)(2,1)S(1)}, bf16[27,32,128]{2,1,0:T(8,128)(2,1)}, u32[]{:S(2)}) %copy-start.1) | copy-done | bytes 221208
  2.8 0.0 copy-start.2
  2.8 0.9 %copy-done.2 = bf16[27,32,128]{2,1,0:T(8,128)(2,1)S(1)} copy-done((bf16[27,32,128]{2,1,0:T(8,128)(2,1)S(1)}, bf16[27,32,128]{2,1,0:T(8,128)(2,1)}, u32[]{:S(2)}) %copy-start.2) | copy-done | bytes 221208
  3.7 0.0 copy-start.3
  3.7 0.9 %copy-done.3 = bf16[2,8,32,128]{3,2,1,0:T(8,128)(2,1)S(1)} copy-done((bf16[2,8,32,128]{3,2,1,0:T(8,128)(2,1)S(1)}, bf16[2,8,32,128]{3,2,1,0:T(8,128)(2,1)}, u32[]{:S(2)}) %copy-start.3) | copy-done | bytes 131096
  4.6 40.5 %shard_map.67 = (bf16[2,8,32,128]{3,2,1,0:T(8,128)(2,1)S(1)}, f32[216,128]{1,0:T(8,128)S(1)}, f32[216,128]{1,0:T(8,128)S(1)}) custom-call(bf16[4,16,64,128]{3,2,1,0:T(8,128)(2,1)S(1)} %copy-done, bf16[27,32,128]{2,1,0:T(8,128)(2,1)S(1)} %copy-done.1, bf16[27,32,128]{2,1,0:T(8,128)(2,1)S(1)} %copy-done.2, bf16[2,8,32,128]{3,2,1,0:T(8,128)(2,1)S(1)} %copy-done.3), custom_call_target="tpu_custom_call" | custom-call | flops 2264924160 | bytes 4194304 | tf_op jit(solution)/shard_map/pallas_call | solution.py:408
  45.1 0.7 %copy.10 = bf16[2,8,32,128]{3,2,1,0:T(8,128)(2,1)} copy(bf16[2,8,32,128]{3,2,1,0:T(8,128)(2,1)S(1)} %get-tuple-element.12) | data formatting | bytes 262144
  45.8 0.7 %copy.11 = f32[27648]{0:T(1024)} copy(f32[27648]{0:T(1024)S(1)} %bitcast.3) | data formatting | bytes 221184
  46.4 0.7 %copy.12 = f32[27648]{0:T(1024)} copy(f32[27648]{0:T(1024)S(1)} %bitcast.2) | data formatting | bytes 221184
Async XLA Ops:
  0.6 1.2 %copy-start = (bf16[4,16,64,128]{3,2,1,0:T(8,128)(2,1)S(1)}, bf16[4,16,64,128]{3,2,1,0:T(8,128)(2,1)}, u32[]{:S(2)}) copy-start(bf16[4,16,64,128]{3,2,1,0:T(8,128)(2,1)} %vol.1) | copy-start | bytes 3145732
  1.9 0.9 %copy-start.1 = (bf16[27,32,128]{2,1,0:T(8,128)(2,1)S(1)}, bf16[27,32,128]{2,1,0:T(8,128)(2,1)}, u32[]{:S(2)}) copy-start(bf16[27,32,128]{2,1,0:T(8,128)(2,1)} %k1.1) | copy-start | bytes 663556
  2.8 0.9 %copy-start.2 = (bf16[27,32,128]{2,1,0:T(8,128)(2,1)S(1)}, bf16[27,32,128]{2,1,0:T(8,128)(2,1)}, u32[]{:S(2)}) copy-start(bf16[27,32,128]{2,1,0:T(8,128)(2,1)} %k2.1) | copy-start | bytes 663556
  3.7 0.9 %copy-start.3 = (bf16[2,8,32,128]{3,2,1,0:T(8,128)(2,1)S(1)}, bf16[2,8,32,128]{3,2,1,0:T(8,128)(2,1)}, u32[]{:S(2)}) copy-start(bf16[2,8,32,128]{3,2,1,0:T(8,128)(2,1)} %cot.1) | copy-start | bytes 393220

commit v2 on v1

--- a/solution.py
+++ b/solution.py
@@ -26,6 +26,10 @@
         src_ref=src, dst_ref=dst, send_sem=send, recv_sem=recv,
         device_id=device, device_id_type=MESH,
     )
+
+
+def beside(at, count):
+    return (at + count - 2) // (count - 1) + (2 * count - 3 - at) // (count - 1)
 
 
 class Rim:
@@ -123,7 +127,7 @@
 
 
 class Scatter:
-    def __init__(self, total, bufs, sems, place):
+    def __init__(self, total, bufs, sems, place, offset, rows):
         inline, xline, inlines, _ = place
         self.total, self.place = total, place
         self.p, self.r1, self.q, self.r2, self.s, self.r3 = bufs
@@ -131,7 +135,8 @@
         self.core, self.x = lax.rem(xline, 2), xline // 2
         near = xline + 1 - 2 * self.core
         far = lax.rem(xline + 2, 4)
-        self.rows = TAPS * LANES // (4 * inlines)
+        self.stride = TAPS * LANES // (4 * inlines)
+        self.offset, self.rows = offset, rows
         self.one = remote(self.p.at[1 - self.core], self.r1, send.at[0], recv.at[0], {"xline": near})
         self.two = remote(self.q.at[1 - self.x], self.r2, send.at[1], recv.at[1], {"xline": far})
         self.three = []
@@ -145,7 +150,7 @@
         slot_rows = self.p.shape[3]
         for slot in range(4 * self.place[2]):
             self.p[slot % 2, slot // 2 % 2, slot // 4] = self.total[
-                pl.ds(slot * self.rows, slot_rows), :
+                pl.ds(slot * self.stride + self.offset, slot_rows), :
             ].astype(BF16)
         self.one.start()
 
@@ -167,13 +172,18 @@
         for n, copy in enumerate(self.three):
             copy.wait_recv()
             total = total + self.r3[n].astype(F32)
-        out[...] = total[: self.rows]
+        out[pl.ds(self.offset, self.rows), :] = total[: self.rows]
 
     def sent(self):
         self.one.wait_send()
         self.two.wait_send()
         for copy in self.three:
             copy.wait_send()
+
+
+def chunks_of(rows):
+    half = -(-rows // 32) * 16
+    return [(0, half), (half, rows - half)] if half < rows else [(0, rows)]
 
 
 def spread_depth(padded, wide, turned, shape):
@@ -190,7 +200,7 @@
 
 def kernel(
     sizes, fused,
-    vol, k1, k2, cot, latent, out1, out2,
+    vol_hbm, k1_hbm, k2_hbm, cot_hbm, latent, out1, out2, vol, k1, k2, cot, load,
     vpad, vwide, fine, cpad, cwide, hpad, hwide, w1, w2, pre, bpre, g1, g2,
     vs, vr, cs, cr, hs, hr, w1s, w1r, w1l, w2s, w2r, w2l, *rest,
 ):
@@ -200,19 +210,45 @@
     rows, cols, depth = cot.shape[0], cot.shape[1], cot.shape[2]
     count = cols * depth
 
+    loads = [
+        pltpu.make_async_copy(src, dst, load.at[n])
+        for n, (src, dst) in enumerate(
+            ((vol_hbm, vol), (k1_hbm, k1), (cot_hbm, cot), (k2_hbm, k2))
+        )
+    ]
+    for copy in loads:
+        copy.start()
+
     barrier = pltpu.get_barrier_semaphore()
     if fused:
-        for di in range(inlines):
-            for dx in range(xlines):
-                if di or dx:
-                    pl.semaphore_signal(
-                        barrier, inc=1, device_id_type=MESH,
-                        device_id={
-                            "inline": lax.rem(inline + di, inlines),
-                            "xline": lax.rem(xline + dx, xlines),
-                        },
-                    )
-        pl.semaphore_wait(barrier, inlines * xlines - 1)
+        def hello(di, dx):
+            pl.semaphore_signal(
+                barrier, inc=1, device_id_type=MESH,
+                device_id={
+                    "inline": lax.rem(inline + di + inlines, inlines),
+                    "xline": lax.rem(xline + dx + xlines, xlines),
+                },
+            )
+
+        corners = [
+            (
+                di, dx,
+                jnp.logical_and(
+                    inline < inlines - 1 if di > 0 else inline > 0,
+                    xline < xlines - 1 if dx > 0 else xline > 0,
+                ),
+            )
+            for di, dx in ALL_WAYS if di and dx
+        ]
+        for di in range(1, inlines):
+            hello(di, 0)
+        for dx in range(1, xlines):
+            hello(0, dx)
+        for di, dx, has in corners:
+            pl.when(has)(functools.partial(hello, di, dx))
+        pl.semaphore_wait(
+            barrier, inlines + xlines - 2 + beside(inline, inlines) * beside(xline, xlines)
+        )
     else:
         def greet(di, first):
             for dx in range(first, xlines):
@@ -225,22 +261,17 @@
                 )
 
         greet(0, 1)
-        pl.semaphore_wait(barrier, xlines - 1)
         for di, has in ((1, inline < inlines - 1), (-1, inline > 0)):
             pl.when(has)(functools.partial(greet, di, 0))
-        for has in (inline < inlines - 1, inline > 0):
-            @pl.when(has)
-            def _():
-                pl.semaphore_wait(barrier, xlines)
+        pl.semaphore_wait(barrier, xlines - 1 + xlines * beside(inline, inlines))
 
     volume_rim = Rim(vol, vpad, 1, vs, vr, UP_WAYS, place)
     cot_rim = Rim(cot, cpad, 1, cs, cr, ALL_WAYS, place)
     first = Spread(k1, w1, (w1s, w1r, w1l), place)
     second = Spread(k2, w2, (w2s, w2r, w2l), place)
-    volume_rim.start()
-    first.start()
-    cot_rim.start()
-    second.start()
+    for copy, group in zip(loads, (volume_rim, first, cot_rim, second)):
+        copy.wait()
+        group.start()
 
     volume_rim.clear()
     cot_rim.clear()
@@ -299,9 +330,17 @@
     second.forward()
 
     if fused:
-        bufs, sems = rest[:12], rest[12:]
-        sum2 = Scatter(g2, bufs[:6], sems[:2], place)
-        sum1 = Scatter(g1, bufs[6:], sems[2:], place)
+        parts = chunks_of(TAPS * LANES // (inlines * xlines))
+        cut = len(parts)
+        bufs, sems = rest[: 12 * cut], rest[12 * cut :]
+        sums = [
+            Scatter(
+                (g2, g1)[n // cut], bufs[6 * n : 6 * n + 6], sems[2 * n : 2 * n + 2], place,
+                *parts[n % cut],
+            )
+            for n in range(2 * cut)
+        ]
+        sum2, sum1 = sums[:cut], sums[cut:]
         pad = g1.shape[0] - TAPS * LANES
         for g in (g1, g2):
             g[TAPS * LANES :, :] = jnp.zeros((pad, LANES), F32)
@@ -317,7 +356,8 @@
         for c in range(3):
             g2[pl.ds((9 * a + 3 * b + c) * LANES, LANES), :] = total[:, c * LANES : (c + 1) * LANES]
     if fused:
-        sum2.first()
+        for part in sum2:
+            part.first()
 
     second.arrive()
     for i in range(rows):
@@ -332,7 +372,8 @@
         sigma = 1.0 / (1.0 + jnp.exp(-value))
         bpre[i] = (total * sigma * (1.0 + value * (1.0 - sigma))).astype(BF16)
     if fused:
-        sum2.second()
+        for part in sum2:
+            part.second()
 
     for a, b in steps:
         total = jnp.zeros((3 * LANES, LANES), F32)
@@ -340,13 +381,16 @@
             total = total + dot(fine_taps(i, a, b), bpre[i], ((0,), (0,)))
         g1[pl.ds((9 * a + 3 * b) * LANES, 3 * LANES), :] = total
     if fused:
-        sum1.first()
-        sum2.third()
+        for part in sum1:
+            part.first()
+        for part in sum2:
+            part.third()
 
     hidden_rim.arrive()
     spread_depth(hpad, hwide, False, (rows, cols, depth))
     if fused:
-        sum1.second()
+        for part in sum1:
+            part.second()
     for i in range(rows):
         total = jnp.zeros((count, LANES), F32)
         for a, b in steps:
@@ -355,11 +399,16 @@
         latent[i] = total.astype(BF16).reshape(cols, depth, LANES)
 
     if fused:
-        sum1.third()
-        sum2.last(out2)
-        sum1.last(out1)
-        sum1.sent()
-        sum2.sent()
+        for part in sum1:
+            part.third()
+        for part in sum2:
+            part.last(out2)
+        for part in sum1:
+            part.last(out1)
+        for part in sum1:
+            part.sent()
+        for part in sum2:
+            part.sent()
     else:
         out1[...] = g1[: TAPS * LANES]
         out2[...] = g2[: TAPS * LANES]
@@ -373,10 +422,14 @@
     shards = inlines * xlines
     fused = inlines <= 4 and (TAPS * LANES) % (8 * shards) == 0
     out_rows = TAPS * LANES // shards if fused else TAPS * LANES
-    slot = -(-out_rows // 16) * 16
     dma = pltpu.SemaphoreType.DMA
     pad_cells = (rows + 2, cols + 2, depth)
     scratch = [
+        pltpu.VMEM(volume.shape, BF16),
+        pltpu.VMEM(first_kernel.shape, BF16),
+        pltpu.VMEM(second_kernel.shape, BF16),
+        pltpu.VMEM(cotangent.shape, BF16),
+        dma((4,)),
         pltpu.VMEM((2 * rows + 1, 2 * cols + 1, 2 * depth, channels), BF16),
         pltpu.VMEM((2 * rows + 1, 2, cols + 1, depth, 3 * channels), BF16),
         pltpu.VMEM((2 * cols + 1, 2 * depth + 8, channels), F32),
@@ -394,7 +447,8 @@
         dma((3,)), dma((3,)), dma, dma((3,)), dma((3,)), dma,
     ]
     if fused:
-        for _ in range(2):
+        for _, chunk in chunks_of(out_rows) * 2:
+            slot = -(-chunk // 16) * 16
             scratch += [
                 pltpu.VMEM((2, 2, inlines, slot, channels), BF16),
                 pltpu.VMEM((2, inlines, slot, channels), BF16),
@@ -403,7 +457,7 @@
                 pltpu.VMEM((inlines, slot, channels), BF16),
                 pltpu.VMEM((max(inlines - 1, 1), slot, channels), BF16),
             ]
-        scratch += [dma((inlines + 1,))] * 4
+        scratch += [dma((inlines + 1,))] * (4 * len(chunks_of(out_rows)))
     flops = 10 * TAPS * channels * channels * rows * cols * depth
     latent, grad1, grad2 = pl.pallas_call(
         functools.partial(kernel, (inlines, xlines), fused),
@@ -412,7 +466,7 @@
             jax.ShapeDtypeStruct((out_rows, channels), F32),
             jax.ShapeDtypeStruct((out_rows, channels), F32),
         ],
-        in_specs=[pl.BlockSpec(memory_space=pltpu.VMEM)] * 4,
+        in_specs=[pl.BlockSpec(memory_space=pltpu.HBM)] * 4,
         out_specs=[pl.BlockSpec(memory_space=pltpu.VMEM)] * 3,
         scratch_shapes=scratch,
         cost_estimate=pl.CostEstimate(flops=flops, bytes_accessed=4 << 20, transcendentals=0),

time: 47.3 us -> 46.3 us (0.979)
  Pallas kernels: 40.5 us -> 39.5 us
    pallas_call x1, Pallas kernels: 40.5 us -> 39.5 us  [local(): pl.pallas_call(functools.partial(kernel, (inlines, xlines), fused), out_s...]
where the time goes in v2:
time: 46.3 us; the launch traced here: 46.1 us
  Pallas kernels  39.5 us (85%)
  local copies, waits for them, and re-layouts  5.95 us (13%)
  between operations  0.65 us (1%)
    pallas_call x1, Pallas kernels, local(): pl.pallas_call(functools.partial(kernel, (inlines, xlines), fused), out_s...  39.5 us
    unnamed x11, local copies, waits for them, and re-layouts  5.95 us

profile of v2, /device:TPU:0, one launch (start us, length us, event | category | flops | bytes accessed | tf_op | source)
XLA Modules:
  0.0 46.1 jit_solution(13170456905348474459)
XLA Ops:
  0.6 0.0 copy-start
  0.6 1.2 %copy-done = bf16[4,16,64,128]{3,2,1,0:T(8,128)(2,1)S(1)} copy-done((bf16[4,16,64,128]{3,2,1,0:T(8,128)(2,1)S(1)}, bf16[4,16,64,128]{3,2,1,0:T(8,128)(2,1)}, u32[]{:S(2)}) %copy-start) | copy-done | bytes 1048600
  1.9 0.0 copy-start.1
  1.9 0.9 %copy-done.1 = bf16[27,32,128]{2,1,0:T(8,128)(2,1)S(1)} copy-done((bf16[27,32,128]{2,1,0:T(8,128)(2,1)S(1)}, bf16[27,32,128]{2,1,0:T(8,128)(2,1)}, u32[]{:S(2)}) %copy-start.1) | copy-done | bytes 221208
  2.8 0.0 copy-start.2
  2.8 0.9 %copy-done.2 = bf16[27,32,128]{2,1,0:T(8,128)(2,1)S(1)} copy-done((bf16[27,32,128]{2,1,0:T(8,128)(2,1)S(1)}, bf16[27,32,128]{2,1,0:T(8,128)(2,1)}, u32[]{:S(2)}) %copy-start.2) | copy-done | bytes 221208
  3.7 0.0 copy-start.3
  3.7 0.9 %copy-done.3 = bf16[2,8,32,128]{3,2,1,0:T(8,128)(2,1)S(1)} copy-done((bf16[2,8,32,128]{3,2,1,0:T(8,128)(2,1)S(1)}, bf16[2,8,32,128]{3,2,1,0:T(8,128)(2,1)}, u32[]{:S(2)}) %copy-start.3) | copy-done | bytes 131096
  4.6 39.5 %shard_map.67 = (bf16[2,8,32,128]{3,2,1,0:T(8,128)(2,1)S(1)}, f32[216,128]{1,0:T(8,128)S(1)}, f32[216,128]{1,0:T(8,128)S(1)}) custom-call(bf16[4,16,64,128]{3,2,1,0:T(8,128)(2,1)S(1)} %copy-done, bf16[27,32,128]{2,1,0:T(8,128)(2,1)S(1)} %copy-done.1, bf16[27,32,128]{2,1,0:T(8,128)(2,1)S(1)} %copy-done.2, bf16[2,8,32,128]{3,2,1,0:T(8,128)(2,1)S(1)} %copy-done.3), custom_call_target="tpu_custom_call" | custom-call | flops 2264924160 | bytes 4194304 | tf_op jit(solution)/shard_map/pallas_call | solution.py:462
  44.1 0.7 %copy.10 = bf16[2,8,32,128]{3,2,1,0:T(8,128)(2,1)} copy(bf16[2,8,32,128]{3,2,1,0:T(8,128)(2,1)S(1)} %get-tuple-element.12) | data formatting | bytes 262144
  44.8 0.7 %copy.11 = f32[27648]{0:T(1024)} copy(f32[27648]{0:T(1024)S(1)} %bitcast.3) | data formatting | bytes 221184
  45.4 0.7 %copy.12 = f32[27648]{0:T(1024)} copy(f32[27648]{0:T(1024)S(1)} %bitcast.2) | data formatting | bytes 221184
Async XLA Ops:
  0.6 1.2 %copy-start = (bf16[4,16,64,128]{3,2,1,0:T(8,128)(2,1)S(1)}, bf16[4,16,64,128]{3,2,1,0:T(8,128)(2,1)}, u32[]{:S(2)}) copy-start(bf16[4,16,64,128]{3,2,1,0:T(8,128)(2,1)} %vol_hbm.1) | copy-start | bytes 3145732
  1.9 0.9 %copy-start.1 = (bf16[27,32,128]{2,1,0:T(8,128)(2,1)S(1)}, bf16[27,32,128]{2,1,0:T(8,128)(2,1)}, u32[]{:S(2)}) copy-start(bf16[27,32,128]{2,1,0:T(8,128)(2,1)} %k1_hbm.1) | copy-start | bytes 663556
  2.8 0.9 %copy-start.2 = (bf16[27,32,128]{2,1,0:T(8,128)(2,1)S(1)}, bf16[27,32,128]{2,1,0:T(8,128)(2,1)}, u32[]{:S(2)}) copy-start(bf16[27,32,128]{2,1,0:T(8,128)(2,1)} %k2_hbm.1) | copy-start | bytes 663556
  3.7 0.9 %copy-start.3 = (bf16[2,8,32,128]{3,2,1,0:T(8,128)(2,1)S(1)}, bf16[2,8,32,128]{3,2,1,0:T(8,128)(2,1)}, u32[]{:S(2)}) copy-start(bf16[2,8,32,128]{3,2,1,0:T(8,128)(2,1)} %cot_hbm.1) | copy-start | bytes 393220
